TPU v7x, 32 devices: a whole 2x2x4 slice. The times are simulated.
32 devices in a mesh: row: 8 (over z, x), col: 4 (over y, core).
Axes of the slice: x: 2, y: 2, z: 4, core: 2. Of those that a mesh axis runs over, the one named last changes fastest.
Arguments:
- front: float32 [12, 1024, 24, 512], P(None, 'row', None, 'col')
- children: float32 [32768, 8192], P('row', 'col')
- block_map: int32 [4, 64], replicated, may hold values from -1 to 95, as said below
- child_at: int32 [4], replicated, may hold values from 0 to 3, each once
Outputs:
- factored: float32 [12, 1024, 24, 512], P(None, 'row', None, 'col')
Inputs may be any that keep to these rules, and one draw needn't show every extreme that they name: Entry block_map[k, t * 8 + p] is -1 or a parent block b with b % 8 == p. For each child k and each p the entries that are not -1 come first in t, increase, and number 8 // 2 to 8; for every child both of these counts occur. No block appears twice for one child. `child_at`: each child stands in exactly one slot.
All inputs are finite; a program needn't handle non-finite values.
Results may differ from a plain program's by a relative error of at most 0.00005.
Values sent between devices are 32-bit elements; how exact they have to be, the bound alone decides.
No kernel may reach another device: no remote copies, remote signals or barrier semaphores. Data moves between devices by JAX's collectives and lax.ppermute only.
A program may use at most 256 MiB of HBM per device.

v0:
```python
import jax
import jax.numpy as jnp
from jax import lax
from jax.sharding import PartitionSpec as P

CHILD = 4
PB = 8


HIGHEST_PRECISION = lax.Precision.HIGHEST


def from_root(value, axis, root):
    mine = lax.axis_index(axis) == root
    return lax.psum(jnp.where(mine, value, jnp.zeros_like(value)), axis)


def widen_columns(local_rows, col_onehot, row_index, per_device, slot_cap):
    owners = (row_index * per_device + jnp.arange(per_device)) // slot_cap
    chosen = jnp.take(col_onehot, owners, axis=0)
    return jnp.einsum("lpxsy,lsb->lpxby", local_rows, chosen, precision=HIGHEST_PRECISION)


def body(front, children, block_map, child_at):
    grid_rows = lax.axis_size("row")
    grid_cols = lax.axis_size("col")
    row_index = lax.axis_index("row")
    col_index = lax.axis_index("col")
    tile_rows = front.shape[0]
    block_size = front.shape[1]
    tile_cols = front.shape[2]
    slot_cap = block_map.shape[1] // grid_rows
    fanout = grid_rows // grid_cols
    group_cap = slot_cap * fanout
    per_device = CHILD * slot_cap // grid_rows
    panel_width = PB * block_size
    panel_tiles = (PB + grid_cols - 1) // grid_cols
    diag_tiles = (PB + grid_rows - 1) // grid_rows
    slot_maps = jnp.take(block_map, child_at, axis=0)
    own_maps = jnp.take(slot_maps.reshape(CHILD, slot_cap, grid_rows), row_index, axis=2)
    row_onehot = (
        (own_maps[:, :, None] >= 0)
        & (own_maps[:, :, None] // grid_rows == jnp.arange(tile_rows)[None, None, :])
    ).astype(jnp.float32)
    columns = jnp.take(slot_maps.reshape(CHILD, slot_cap, fanout, grid_cols), col_index, axis=3)
    columns = columns.transpose(0, 2, 1).reshape(CHILD, group_cap)
    col_onehot = (
        (columns[:, :, None] >= 0)
        & (columns[:, :, None] // grid_cols == jnp.arange(tile_cols)[None, None, :])
    ).astype(jnp.float32)
    local_rows = children.reshape(per_device, grid_rows, block_size, group_cap, block_size)
    assembled = None
    widened = widen_columns(local_rows, col_onehot, row_index, per_device, slot_cap)
    received = lax.all_to_all(widened, "row", split_axis=1, concat_axis=0, tiled=True)
    shaped = received.reshape(CHILD, slot_cap, received.shape[2], received.shape[3], block_size)
    assembled = front + jnp.einsum(
        "cta,ctxby->axby", row_onehot, shaped, precision=HIGHEST_PRECISION
    )
    panel_part = assembled[:, :, :panel_tiles]
    gathered = lax.all_gather(
        panel_part.reshape(tile_rows * block_size, panel_tiles, 1, block_size),
        "col",
        axis=2,
        tiled=True,
    )
    panel_rows = gathered.reshape(tile_rows * block_size, panel_tiles * grid_cols * block_size)
    picked = panel_rows.reshape(tile_rows, block_size, panel_width)[:diag_tiles][:, None]
    stacked = lax.all_gather(picked, "row", axis=1, tiled=True)
    corner = stacked.reshape(diag_tiles * grid_rows * block_size, panel_width)[:panel_width]
    factor = jnp.linalg.cholesky(0.5 * (corner + corner.T))
    solved = jax.scipy.linalg.solve_triangular(factor, panel_rows.T, lower=True).T
    global_rows = (
        jnp.arange(tile_rows)[:, None] * grid_rows + row_index
    ) * block_size + jnp.arange(block_size)[None, :]
    flat_rows = global_rows.reshape(-1)
    top_rows = jnp.take(factor, jnp.clip(flat_rows, 0, panel_width - 1), axis=0)
    panel_out = jnp.where((flat_rows < panel_width)[:, None], top_rows, solved)
    pieces = []
    for offset in range(fanout):
        pieces.append(
            from_root(
                solved.reshape(tile_rows, block_size, panel_width),
                "row",
                col_index + offset * grid_cols,
            )
        )
    across = jnp.stack(pieces, axis=1).reshape(tile_cols * block_size, panel_width)
    product = jnp.dot(solved, across.T, precision=HIGHEST_PRECISION).reshape(
        tile_rows, block_size, tile_cols, block_size
    )
    global_cols = (
        jnp.arange(tile_cols)[:, None] * grid_cols + col_index
    ) * block_size + jnp.arange(block_size)[None, :]
    inside = (global_rows >= panel_width)[:, :, None, None] & (global_cols >= panel_width)[
        None, None, :, :
    ]
    updated = jnp.where(inside, assembled - product, assembled)
    head_cols = global_cols[:panel_tiles].reshape(-1)
    head_part = jnp.take(panel_out, jnp.clip(head_cols, 0, panel_width - 1), axis=1).reshape(
        tile_rows, block_size, panel_tiles, block_size
    )
    head_part = jnp.where(
        (global_cols[:panel_tiles] < panel_width)[None, None],
        head_part,
        updated[:, :, :panel_tiles],
    )
    return jnp.concatenate([head_part, updated[:, :, panel_tiles:]], axis=2)


def solution(mesh):
    in_specs = (P(None, "row", None, "col"), P("row", "col"), P(), P())
    out_specs = P(None, "row", None, "col")
    return jax.shard_map(body, mesh=mesh, in_specs=in_specs, out_specs=out_specs, check_vma=False)
```

profile of v0, /device:TPU:19, one launch (start us, length us, event | category | flops | bytes accessed | tf_op | source)
XLA Modules:
  0.0 2344.1 jit_solution(14796664316062025736)
XLA Ops:
  9.0 27.6 %copy.82 = f32[512,8,16,128]{3,2,1,0:T(8,128)} copy(f32[512,8,16,128]{3,1,2,0:T(8,128)} %bitcast.207) | data formatting | bytes 67108864
  37.9 46.8 %convolution_bitcast_fusion = f32[4,8,128,24,128]{4,3,2,1,0:T(8,128)} fusion(f32[4,8,128,16,128]{4,3,2,1,0:T(8,128)} %bitcast.206, f32[4,16,24]{2,1,0:T(8,128)S(1)} %gather_fusion.1, pred[4]{0:T(512)(128)(4,1)S(1)} %get-tuple-element.108), kind=kOutput, calls=%fused_computation.11 | convolution fusion | flops 2415920640 | bytes 83892224 | tf_op jit(solution)/shard_map/lpxsy,lsb->lpxby/dot_general | solution.py:21
  84.7 34.1 %copy.56 = f32[4,8,128,24,128]{4,3,2,0,1:T(8,128)} copy(f32[4,8,128,24,128]{4,3,2,1,0:T(8,128)} %convolution_bitcast_fusion) | data formatting | bytes 100663296 | tf_op jit(solution)/shard_map/lpxsy,lsb->lpxby/transpose | solution.py:21
  118.8 8.5 all-to-all-start
  128.1 1077.8 %all-to-all-done = f32[4,8,128,24,128]{4,3,2,0,1:T(8,128)} async-done(((f32[4,8,128,24,128]{4,3,2,0,1:T(8,128)}), f32[4,8,128,24,128]{4,3,2,0,1:T(8,128)}, u32[]{:S(2)}, u32[]{:S(2)}) %all-to-all-start) | async-done | bytes 50331680 | tf_op jit(solution)/shard_map/all_to_all | solution.py:54
  1205.9 69.7 %bitcast_add_fusion = f32[12,128,24,128]{3,0,2,1:T(8,128)} fusion(f32[12,128,24,128]{3,2,1,0:T(8,128)} %param.4, f32[4,8,128,24,128]{4,3,2,1,0:T(8,128)} %bitcast.13, pred[4,8,12,1,1]{2,1,0,4,3:T(8,128)(4,1)S(1)} %fusion.122), kind=kOutput, calls=%fused_computation.10 | convolution fusion | flops 1816657920 | bytes 88080768 | tf_op jit(solution)/shard_map/cta,ctxby->axby/dot_general | solution.py:56
  1279.3 49.4 %all-gather.3.cloned.1.call-done = f32[1536,2,4,128]{3,0,1,2:T(8,128)} async-done(((f32[1536,2,1,128]{3,0,1,2:T(8,128)}), f32[1536,2,4,128]{3,0,1,2:T(8,128)}) %all-gather.3.cloned.1.call-update) | async-done | bytes 6291472 | tf_op jit(solution)/shard_map/all_gather | solution.py:60
  1328.7 6.6 copy.60
  1337.5 70.9 %all-gather.5.cloned.1.call-done = f32[1,8,128,1024]{3,2,0,1:T(8,128)} async-done(((f32[1,1,128,1024]{3,2,0,1:T(8,128)}), f32[1,8,128,1024]{3,2,0,1:T(8,128)}) %all-gather.5.cloned.1.call-update) | async-done | bytes 4194320 | tf_op jit(solution)/shard_map/all_gather | solution.py:68
  1408.4 5.4 copy.78
  1413.7 6.9 fusion.5
  1420.6 5.7 copy.64
  1426.3 4.4 fusion.4
  1432.7 11.7 cholesky.223
  1447.0 9.8 custom-call.63
  1460.7 11.9 cholesky.244
  1473.2 9.8 custom-call.64
  1486.4 11.7 cholesky.468
  1498.7 9.8 custom-call.65
  1512.1 11.9 cholesky.487
  1524.6 9.8 custom-call.66
  1537.9 11.7 cholesky.506
  1550.3 10.2 custom-call.67
  1563.8 11.7 cholesky.526
  1576.1 9.8 custom-call.68
  1588.9 11.7 cholesky.546
  1601.5 9.8 custom-call.69
  1613.9 11.7 cholesky.564
  1636.8 6.6 fusion.6
  1643.5 22.5 while.3
  1665.9 78.8 %custom-call.70 = f32[8,128,128]{1,2,0:T(8,128)S(1)} custom-call(f32[8,128,128]{2,1,0:T(8,128)S(1)} %get-tuple-element.28), custom_call_target="InvertDiagBlocksLowerTriangular" | custom-call | tf_op jit(solution)/shard_map/jit(_solve_triangular)/triangular_solve | solution.py:71
  1765.0 3.8 convolution_subtract_fusion.2
  1770.6 3.7 convolution_subtract_fusion.5
  1776.0 4.3 convolution_subtract_fusion.1
  1782.1 6.6 copy.70
  1788.7 9.8 select_bitcast_fusion.1
  1799.9 10.0 gather_fusion.2
  1809.9 6.8 copy.65
  1816.6 8.8 select_select_fusion
  1825.4 6.0 gather_fusion.3
  1835.3 361.1 %all-reduce.4.cloned.1.call-done = (f32[12,1,128,1024]{3,2,0,1:T(8,128)}, f32[12,1,128,1024]{3,2,0,1:T(8,128)}) async-done(((f32[12,1,128,1024]{3,2,0,1:T(8,128)}, f32[12,1,128,1024]{3,2,0,1:T(8,128)}), (f32[12,1,128,1024]{3,2,0,1:T(8,128)}, f32[12,1,128,1024]{3,2,0,1:T(8,128)})) %all-reduce.4.cloned.1.call-update) | async-done | bytes 12582928 | tf_op jit(solution)/shard_map/psum | solution.py:15
  2196.5 12.3 pad_maximum_fusion.1
  2208.8 12.0 copy.71
  2220.8 65.1 %fusion.100 = f32[12,128,24,128]{3,1,2,0:T(8,128)} fusion(f32[12,128,1024,1]{2,1,3,0:T(8,128)S(1)} %bitcast.211, f32[24,128,1024,1]{2,1,0,3:T(8,128)} %bitcast.223), kind=kOutput, calls=%fused_computation.248 | convolution fusion | flops 57982058496 | bytes 37748736 | tf_op jit(solution)/shard_map/dot_general | solution.py:88
  2285.9 21.0 subtract_select_fusion
  2307.0 8.5 slice.311
  2316.0 9.3 pad_maximum_fusion
  2325.3 12.0 copy.73
  (149 shorter events, 101.6 us)
Async XLA Ops:
  6.5 0.7 copy-start
  8.9 27.6 %copy-start.5 = (s32[24]{0:T(128)}, s32[24]{0:T(128)S(1)}, u32[]{:S(2)}) copy-start(s32[24]{0:T(128)S(1)} %add_multiply_fusion.1) | copy-start | bytes 292
  36.6 0.7 copy-start.4
  118.8 1087.1 %all-to-all-start = ((f32[4,8,128,24,128]{4,3,2,0,1:T(8,128)}), f32[4,8,128,24,128]{4,3,2,0,1:T(8,128)}, u32[]{:S(2)}, u32[]{:S(2)}) async-start(f32[4,8,128,24,128]{4,3,2,0,1:T(8,128)} %copy.56), calls=%async_computation | async-start | bytes 100663296 | tf_op jit(solution)/shard_map/all_to_all | solution.py:54
  127.3 1201.4 %all-gather.3.cloned.1.call-start = ((), (), s32[]{:S(2)}) async-start(), calls=%async_computation.1 | async-start | bytes 7864320 | tf_op jit(solution)/shard_map/all_gather | solution.py:60
  1275.6 1.6 slice-start
  1279.3 129.1 %all-gather.5.cloned.1.call-start = ((), (), s32[]{:S(2)}) async-start(), calls=%async_computation.2 | async-start | bytes 4718592 | tf_op jit(solution)/shard_map/all_gather | solution.py:68
  1337.4 859.1 %all-reduce.4.cloned.1.call-start = ((), (), s32[]{:S(2)}) async-start(), calls=%async_computation.3 | async-start | bytes 25165824 | tf_op jit(solution)/shard_map/psum | solution.py:15
  1430.8 1.9 copy-start.2
  1749.7 6.2 slice-start.3
  1751.6 4.3 slice-start.4
  1798.4 0.7 copy-start.6
  2196.5 24.3 %slice-start.1 = ((s8[6291456]{0:T(1024)(128)(4,1)}), s8[4194304]{0:T(1024)(128)(4,1)S(1)}, s32[]{:S(2)}) async-start(s8[6291456]{0:T(1024)(128)(4,1)} %bitcast.209), calls=%async_computation.5 | async-start | bytes 8388608
  2208.8 12.0 slice-start.2
  2306.9 8.5 copy-start.3
  2325.3 12.0 copy-start.1
Sparse Core Ops, SparseCore 0:
  1279.4 49.2 all-gather.2
  1337.5 70.8 all-gather.4
  1798.6 397.8 all-reduce.3
where the time goes:
time: 2350 us; the launch traced here: 2340 us
  waiting for transfers between devices  1560 us (66%)
  other arithmetic  335 us (14%)
  matrix products  242 us (10%)
  local copies, waits for them, and re-layouts  180 us (8%)
    all_to_all x1, waiting for transfers between devices, body(): lax.all_to_all(widened, 'row', split_axis=1, concat_axis=0, tiled=True)  1080 us
    psum x1, waiting for transfers between devices, from_root(): return lax.psum(jnp.where(mine, value, jnp.zeros_like(value)), axis)  361 us
    another operation x31, other arithmetic, body(): factor = jnp.linalg.cholesky(0.5 * (corner + corner.T))  173 us
    another operation x3, other arithmetic, body(): jax.scipy.linalg.solve_triangular(factor, panel_rows.T, lower=True)  85.4 us
    all_gather x1, waiting for transfers between devices, body(): stacked = lax.all_gather(picked, 'row', axis=1, tiled=True)  70.9 us
    dot_general x1, matrix products, body(): jnp.einsum('cta,ctxby->axby', row_onehot, shaped, precision=HIGHEST_PRECI...  69.7 us
    dot_general x1, matrix products, body(): jnp.dot(solved, across.T, precision=HIGHEST_PRECISION)  65.1 us
    all_gather x1, waiting for transfers between devices, body(): lax.all_gather(panel_part.reshape(tile_rows * block_size, panel_tiles, 1,...  49.4 us
  transfers between devices with their start and end apart: 4, of which 4 were waited for; matrix products, arithmetic and copies ran while one was open for 2% of the time, Pallas kernels for 0%

commit v1 on v0

v1 whole, which is shorter than its diff:
```python
import jax
import jax.numpy as jnp
from jax import lax
from jax.experimental import pallas as pl
from jax.experimental.pallas import tpu as pltpu
from jax.sharding import PartitionSpec as P

CHILD = 4
PB = 8
HIGHEST_PRECISION = lax.Precision.HIGHEST
VMEM_LIMIT = 56 * 1024 * 1024


def split_halves(value):
    rounded = lax.reduce_precision(value, exponent_bits=8, mantissa_bits=7)
    return rounded.astype(jnp.bfloat16), (value - rounded).astype(jnp.bfloat16)


def add_slot(out_ref, source_ref, row_count, tile_cols, block, lane_start, block_size):
    for start in range(0, row_count, 8):
        place = pl.ds(start * tile_cols + block, 8, stride=tile_cols)
        out_ref[0, place, :] += source_ref[0, start : start + 8, lane_start : lane_start + block_size]


def base_kernel(
    rows_ref, cols_ref, place_ref, front_ref, own_high, own_low, across_high, across_low, *rest,
    tile_cols, block_size, panel_tiles,
):
    head_refs = rest[:panel_tiles]
    slot_refs = rest[panel_tiles:-1]
    out_ref = rest[-1]
    row_count = own_high.shape[0]
    tile = pl.program_id(0)
    group = 2 if tile_cols % 2 == 0 else 1
    width = group * block_size
    for first in range(0, tile_cols, group):
        lanes = slice(first * block_size, first * block_size + width)
        dims = (((1,), (1,)), ((), ()))
        product = lax.dot_general(
            own_high[...], across_high[lanes, :], dims, preferred_element_type=jnp.float32
        )
        product += lax.dot_general(
            own_high[...], across_low[lanes, :], dims, preferred_element_type=jnp.float32
        )
        product += lax.dot_general(
            own_low[...], across_high[lanes, :], dims, preferred_element_type=jnp.float32
        )
        for offset in range(group):
            block = first + offset
            for start in range(0, row_count, 8):
                place = pl.ds(start * tile_cols + block, 8, stride=tile_cols)
                if block < panel_tiles:
                    out_ref[0, place, :] = head_refs[block][start : start + 8, :]
                else:
                    piece = product[start : start + 8, offset * block_size : (offset + 1) * block_size]
                    out_ref[0, place, :] = front_ref[0, place, :] - piece
    for child in range(CHILD):
        for slot in range(panel_tiles):
            block = cols_ref[child, slot]

            @pl.when((rows_ref[child, tile] >= 0) & (block >= 0))
            def _():
                add_slot(
                    out_ref, slot_refs[child], row_count, tile_cols, block, slot * block_size, block_size
                )


def add_kernel(rows_ref, cols_ref, base_ref, *rest, tile_cols, block_size, slot_count):
    slot_refs = rest[:-1]
    out_ref = rest[-1]
    row_count = slot_refs[0].shape[1]
    tile = pl.program_id(0)
    out_ref[...] = base_ref[...]
    for child in range(CHILD):

        @pl.when(rows_ref[child, tile] >= 0)
        def _():
            for slot in range(slot_count):
                block = cols_ref[child, slot]

                @pl.when(block >= 0)
                def _():
                    add_slot(
                        out_ref, slot_refs[child], row_count, tile_cols, block, slot * block_size, block_size
                    )


def slot_spec(child, rows, width):
    def index(tile, part, rows_ref, *_):
        source = rows_ref[child, tile]
        there = source >= 0
        return jnp.where(there, source, 0), jnp.where(there, part, 0), 0

    return pl.BlockSpec((1, rows, width), index)


def make_base(front, own, across, heads, slots, row_table, col_table, place, panel_tiles, tile_cols):
    tile_rows = front.shape[0]
    block_size = front.shape[2]
    rows = block_size
    depth = own[0].shape[1]
    flat = pl.BlockSpec((1, rows * tile_cols, block_size), lambda a, x, *_: (a, x, 0))
    own_spec = pl.BlockSpec((rows, depth), lambda a, x, *_: (a, 0))
    whole_spec = pl.BlockSpec(across[0].shape, lambda a, x, *_: (0, 0), pipeline_mode=pl.Buffered(1))
    grid_cols = depth // block_size // panel_tiles

    def head_spec(tile):
        return pl.BlockSpec(
            (rows, block_size), lambda a, x, r, c, place_ref: (a, tile * grid_cols + place_ref[0])
        )

    return pl.pallas_call(
        lambda *refs: base_kernel(
            *refs, tile_cols=tile_cols, block_size=block_size, panel_tiles=panel_tiles
        ),
        grid_spec=pltpu.PrefetchScalarGridSpec(
            num_scalar_prefetch=3,
            grid=(tile_rows, 1),
            in_specs=[flat, own_spec, own_spec, whole_spec, whole_spec]
            + [head_spec(tile) for tile in range(panel_tiles)]
            + [slot_spec(child, rows, panel_tiles * block_size) for child in range(CHILD)],
            out_specs=flat,
        ),
        out_shape=jax.ShapeDtypeStruct(front.shape, jnp.float32),
        compiler_params=pltpu.CompilerParams(vmem_limit_bytes=VMEM_LIMIT),
        cost_estimate=pl.CostEstimate(
            flops=6 * tile_rows * rows * depth * across[0].shape[0],
            bytes_accessed=60_000_000,
            transcendentals=0,
        ),
        name="trailing_base",
    )(
        row_table, col_table, place, front, own[0], own[1], across[0], across[1],
        *([heads] * panel_tiles), *([slots] * CHILD),
    )


def make_final(base, slots, row_table, col_table, tile_cols):
    tile_rows = base.shape[0]
    block_size = base.shape[2]
    rows = block_size // 2
    width = slots.shape[2]
    flat = pl.BlockSpec((1, rows * tile_cols, block_size), lambda a, x, *_: (a, x, 0))
    return pl.pallas_call(
        lambda *refs: add_kernel(
            *refs, tile_cols=tile_cols, block_size=block_size, slot_count=width // block_size
        ),
        grid_spec=pltpu.PrefetchScalarGridSpec(
            num_scalar_prefetch=2,
            grid=(tile_rows, block_size // rows),
            in_specs=[flat] + [slot_spec(child, rows, width) for child in range(CHILD)],
            out_specs=flat,
        ),
        out_shape=jax.ShapeDtypeStruct(base.shape, jnp.float32),
        compiler_params=pltpu.CompilerParams(vmem_limit_bytes=VMEM_LIMIT),
        cost_estimate=pl.CostEstimate(flops=0, bytes_accessed=70_000_000, transcendentals=0),
        name="extend_add",
    )(row_table, col_table, base, *([slots] * CHILD))


def body(front, children, block_map, child_at):
    grid_rows = lax.axis_size("row")
    grid_cols = lax.axis_size("col")
    row_index = lax.axis_index("row")
    col_index = lax.axis_index("col")
    tile_rows, block_size, tile_cols, _ = front.shape
    slot_cap = block_map.shape[1] // grid_rows
    fanout = grid_rows // grid_cols
    group_cap = slot_cap * fanout
    per_device = CHILD * slot_cap // grid_rows
    slot_rows = CHILD * slot_cap
    panel_width = PB * block_size
    panel_tiles = (PB + grid_cols - 1) // grid_cols
    diag_tiles = (PB + grid_rows - 1) // grid_rows
    local_rows = tile_rows * block_size
    piece_width = panel_tiles * block_size

    slot_maps = jnp.take(block_map, child_at, axis=0)
    own_maps = jnp.take(slot_maps.reshape(CHILD, slot_cap, grid_rows), row_index, axis=2)
    row_hit = (own_maps[:, :, None] >= 0) & (
        own_maps[:, :, None] // grid_rows == jnp.arange(tile_rows)[None, None, :]
    )
    slot_ids = jnp.arange(slot_rows, dtype=jnp.int32).reshape(CHILD, slot_cap)
    row_table = jnp.max(jnp.where(row_hit, slot_ids[:, :, None], -1), axis=1).astype(jnp.int32)
    columns = jnp.take(slot_maps.reshape(CHILD, slot_cap, fanout, grid_cols), col_index, axis=3)
    columns = columns.transpose(0, 2, 1)
    column_blocks = jnp.where(columns >= 0, columns // grid_cols, -1).astype(jnp.int32)
    in_panel = (columns[:, :panel_tiles, 0] >= 0) & (columns[:, :panel_tiles, 0] < PB)
    early_table = jnp.where(in_panel, -1, column_blocks[:, :panel_tiles, 0])
    late_table = jnp.concatenate(
        [column_blocks[:, j, (1 if j < panel_tiles else 0) :] for j in range(fanout)], axis=1
    )
    place = col_index.astype(jnp.int32).reshape(1)

    def to_rows(parts):
        packed = jnp.concatenate(parts, axis=1)
        packed = packed.reshape(per_device, grid_rows, block_size, packed.shape[1])
        return packed.transpose(1, 0, 2, 3)

    def exchange(packed):
        got = lax.all_to_all(packed, "row", split_axis=0, concat_axis=0, tiled=True)
        return got.reshape(slot_rows, block_size, packed.shape[3])

    span = slot_cap * block_size
    early = exchange(
        to_rows([children[:, j * span : j * span + block_size] for j in range(panel_tiles)])
    )
    late_send = to_rows(
        [
            children[:, j * span + (block_size if j < panel_tiles else 0) : (j + 1) * span]
            for j in range(fanout)
        ]
    )
    lane_mask = jnp.repeat(in_panel, block_size, axis=1).astype(jnp.float32)
    masked = early.reshape(CHILD, slot_cap, block_size, piece_width) * lane_mask[:, None, None, :]
    piece = jnp.einsum(
        "cta,ctxw->axw", row_hit.astype(jnp.float32), masked, precision=HIGHEST_PRECISION
    )
    piece = piece + front[:, :, :panel_tiles].reshape(tile_rows, block_size, piece_width)

    piece = piece.reshape(local_rows, piece_width)
    turn = [
        (g * grid_cols + q, ((g // grid_cols) * grid_cols + q) * grid_cols + g % grid_cols)
        for g in range(grid_rows)
        for q in range(grid_cols)
    ]
    turned = lax.ppermute(piece, ("row", "col"), turn)
    across_panel = lax.all_gather(turned, "row", axis=0, tiled=False)
    piece, across_panel, late_send = lax.optimization_barrier((piece, across_panel, late_send))
    late = exchange(late_send)

    top = across_panel.reshape(fanout, grid_cols, local_rows, piece_width)[
        :, :, : diag_tiles * block_size
    ]
    corner = lax.all_gather(top, "col", axis=0, tiled=False)
    corner = corner.reshape(
        grid_cols, fanout, grid_cols, diag_tiles, block_size, panel_tiles, block_size
    )
    corner = corner.transpose(3, 1, 0, 4, 5, 2, 6).reshape(
        diag_tiles * grid_rows * block_size, panel_width
    )[:panel_width]
    own_panel = lax.all_gather(piece, "col", axis=0, tiled=False)
    across_panel = across_panel.reshape(fanout, grid_cols, local_rows, piece_width)

    factor = jnp.linalg.cholesky(0.5 * (corner + corner.T))
    inverse = jax.scipy.linalg.solve_triangular(
        factor, jnp.eye(panel_width, dtype=jnp.float32), lower=True
    )
    weights = inverse.reshape(panel_width, panel_tiles, grid_cols, block_size)
    weights = weights.transpose(2, 1, 3, 0).reshape(grid_cols, piece_width, panel_width)

    own = jnp.einsum("crw,cwn->rn", own_panel, weights, precision=HIGHEST_PRECISION)
    across = jnp.einsum("fcrw,cwn->frn", across_panel, weights, precision=HIGHEST_PRECISION)

    own = own.reshape(tile_rows, block_size, panel_width)
    own_blocks = jnp.arange(tile_rows) * grid_rows + row_index
    own_below = (own_blocks >= PB)[:, None, None]
    top = lax.dynamic_slice_in_dim(
        factor, jnp.minimum(row_index, PB - 1) * block_size, block_size, axis=0
    )
    heads = jnp.where(own_below, own, top[None]).reshape(local_rows, panel_width)
    own_halves = split_halves(jnp.where(own_below, own, 0.0).reshape(local_rows, panel_width))
    across = across.reshape(fanout, tile_rows, block_size, panel_width).transpose(1, 0, 2, 3)
    across_blocks = jnp.arange(tile_cols) * grid_cols + col_index
    across = jnp.where(
        (across_blocks >= PB)[:, None, None],
        across.reshape(tile_cols, block_size, panel_width),
        0.0,
    )
    across_halves = split_halves(across.reshape(tile_cols * block_size, panel_width))

    flat = front.reshape(tile_rows, block_size * tile_cols, block_size)
    base = make_base(
        flat, own_halves, across_halves, heads, early, row_table, early_table, place,
        panel_tiles, tile_cols,
    )
    result = make_final(base, late, row_table, late_table, tile_cols)
    return result.reshape(front.shape)


def solution(mesh):
    in_specs = (P(None, "row", None, "col"), P("row", "col"), P(), P())
    out_specs = P(None, "row", None, "col")
    return jax.shard_map(body, mesh=mesh, in_specs=in_specs, out_specs=out_specs, check_vma=False)
```

time: 2350 us -> 1020 us (0.43)
  waiting for transfers between devices: 1560 us -> 307 us
  Pallas kernels: 0 us -> 114 us
  matrix products: 242 us -> 129 us
  local copies, waits for them, and re-layouts: 180 us -> 124 us
  other arithmetic: 335 us -> 301 us
    all_to_all x1 -> x2, waiting for transfers between devices: 1080 us -> 101 us  [exchange(): got = lax.all_to_all(packed, 'row', split_axis=0, concat_axis=0, tiled=True)]
    psum x1 -> x0, waiting for transfers between devices: 361 us -> none  [from_root(): return lax.psum(jnp.where(mine, value, jnp.zeros_like(value)), axis)]
    pallas_call x0 -> x2, Pallas kernels: none -> 114 us  [the longest x1 81.4 us: make_base(): pl.pallas_call(lambda *refs: base_kernel(*refs, tile_cols=tile_cols, bloc...]
    dot_general x3, matrix products: 182 us -> 77.4 us  [the longest x1 46.2 us: body(): jnp.einsum('fcrw,cwn->frn', across_panel, weights, precision=HIGHEST_PREC...]
    all_gather x2 -> x3, waiting for transfers between devices: 120 us -> 206 us  [the longest x1 175 us: body(): across_panel = lax.all_gather(turned, 'row', axis=0, tiled=False)]
    select_n x7 -> x2, other arithmetic: 30.4 us -> 0.02 us  [the longest x1 0.01 us: body(): jnp.where(columns >= 0, columns // grid_cols, -1).astype(jnp.int32)]
    gather x6 -> x0, local copies, waits for them, and re-layouts: 27.2 us -> none  [the longest x2 16.7 us: body(): top_rows = jnp.take(factor, jnp.clip(flat_rows, 0, panel_width - 1), axis=0)]
    unnamed x24 -> x18, local copies, waits for them, and re-layouts: 29.9 us -> 4.09 us
  transfers between devices with their start and end apart: 4 -> 6, of which waited for: 4 -> 4; matrix products, arithmetic and copies ran while one was open for 2% -> 53% of each run, Pallas kernels for 0% -> 8%
where the time goes in v1:
time: 1020 us; the launch traced here: 1010 us
  waiting for transfers between devices  307 us (30%)
  other arithmetic  301 us (30%)
  matrix products  129 us (13%)
  local copies, waits for them, and re-layouts  124 us (12%)
  Pallas kernels  114 us (11%)
  between operations  18.6 us (2%)
  starting transfers between devices  15.4 us (2%)
    all_gather x1, waiting for transfers between devices, body(): across_panel = lax.all_gather(turned, 'row', axis=0, tiled=False)  175 us
    another operation x30, other arithmetic, body(): factor = jnp.linalg.cholesky(0.5 * (corner + corner.T))  172 us
    all_to_all x2, waiting for transfers between devices, exchange(): got = lax.all_to_all(packed, 'row', split_axis=0, concat_axis=0, tiled=True)  101 us
    another operation x3, other arithmetic, body(): jax.scipy.linalg.solve_triangular(factor, jnp.eye(panel_width, dtype=jnp....  85.6 us
    pallas_call x1, Pallas kernels, make_base(): pl.pallas_call(lambda *refs: base_kernel(*refs, tile_cols=tile_cols, bloc...  81.4 us
    dot_general x1, matrix products, body(): jnp.einsum('fcrw,cwn->frn', across_panel, weights, precision=HIGHEST_PREC...  46.2 us
    pallas_call x1, Pallas kernels, make_final(): pl.pallas_call(lambda *refs: add_kernel(*refs, tile_cols=tile_cols, block...  32.7 us
    all_gather x1, waiting for transfers between devices, body(): corner = lax.all_gather(top, 'col', axis=0, tiled=False)  31.2 us
  transfers between devices with their start and end apart: 6, of which 4 were waited for; matrix products, arithmetic and copies ran while one was open for 53% of the time, Pallas kernels for 8%

profile of v1, /device:TPU:19, one launch (start us, length us, event | category | flops | bytes accessed | tf_op | source)
XLA Modules:
  0.0 1008.9 jit_solution(4522870249092379112)
XLA Ops:
  11.7 5.7 all-to-all-start
  18.8 3.2 slice.283
  23.4 83.7 %all-to-all-done = f32[8,4,128,256]{3,2,1,0:T(8,128)} async-done(((f32[8,4,128,256]{3,2,1,0:T(8,128)}), f32[8,4,128,256]{3,2,1,0:T(8,128)}, u32[]{:S(2)}, u32[]{:S(2)}) %all-to-all-start) | async-done | bytes 4194336 | tf_op jit(solution)/shard_map/all_to_all | solution.py:201
  107.1 6.1 fusion.15
  116.3 19.6 %fusion.91 = (f32[4096,896]{1,0:T(8,128)}, f32[4096,896]{1,0:T(8,128)}) fusion(f32[4096,2048]{1,0:T(8,128)} %param.5), kind=kLoop, calls=%fused_computation.226 | loop fusion | bytes 58720256 | tf_op jit(solution)/shard_map/slice | solution.py:210
  135.8 10.8 %pad_maximum_fusion = f32[4096,1792]{1,0:T(8,128)S(1)} fusion(f32[4096,896]{1,0:T(8,128)} %get-tuple-element.56, f32[4096,896]{1,0:T(8,128)} %get-tuple-element.55), kind=kLoop, calls=%fused_computation.3 | loop fusion | flops 7340032 | bytes 58720256 | tf_op jit(solution)/shard_map/concatenate | solution.py:196
  146.6 10.0 copy.88
  156.6 175.3 %all-gather.7.cloned.1.call-done = f32[12288,256]{1,0:T(8,128)} async-done(((f32[1536,256]{1,0:T(8,128)}), f32[12288,256]{1,0:T(8,128)}) %all-gather.7.cloned.1.call-update) | async-done | bytes 12582928 | tf_op jit(solution)/shard_map/all_gather | solution.py:228
  331.9 8.7 all-to-all-start.1
  345.6 2.6 fusion.28
  348.4 31.2 %all-gather.11.cloned.1.call-done = f32[8,4,128,256]{3,2,1,0:T(8,128)} async-done(((f32[2,4,128,256]{3,2,1,0:T(8,128)}), f32[8,4,128,256]{3,2,1,0:T(8,128)}) %all-gather.11.cloned.1.call-update) | async-done | bytes 4194320 | tf_op jit(solution)/shard_map/all_gather | solution.py:235
  379.5 5.3 copy.62
  384.8 7.3 copy.63
  392.1 5.6 reshape.241
  397.7 5.4 copy.64
  403.1 7.0 fusion.3
  410.1 5.6 copy.65
  415.6 4.5 fusion.2
  422.1 11.7 %cholesky.223 = f32[128,128]{1,0:T(8,128)S(1)} custom-call(f32[128,128]{1,0:T(8,128)S(1)} %cholesky.580), custom_call_target="Cholesky" | custom-call | tf_op jit(solution)/shard_map/jit(cholesky)/cholesky | solution.py:245
  436.4 9.8 custom-call.63
  450.1 12.1 %cholesky.244 = f32[128,128]{1,0:T(8,128)S(1)} custom-call(f32[128,128]{1,0:T(8,128)S(1)} %cholesky.584), custom_call_target="Cholesky" | custom-call | tf_op jit(solution)/shard_map/jit(cholesky)/cholesky | solution.py:245
  462.8 9.8 custom-call.64
  476.0 11.7 %cholesky.468 = f32[128,128]{1,0:T(8,128)S(1)} custom-call(f32[128,128]{1,0:T(8,128)S(1)} %cholesky.589), custom_call_target="Cholesky" | custom-call | tf_op jit(solution)/shard_map/jit(cholesky)/cholesky | solution.py:245
  488.3 9.8 custom-call.65
  501.7 11.9 %cholesky.487 = f32[128,128]{1,0:T(8,128)S(1)} custom-call(f32[128,128]{1,0:T(8,128)S(1)} %cholesky.594), custom_call_target="Cholesky" | custom-call | tf_op jit(solution)/shard_map/jit(cholesky)/cholesky | solution.py:245
  514.2 9.8 custom-call.66
  527.4 11.7 %cholesky.506 = f32[128,128]{1,0:T(8,128)S(1)} custom-call(f32[128,128]{1,0:T(8,128)S(1)} %cholesky.599), custom_call_target="Cholesky" | custom-call | tf_op jit(solution)/shard_map/jit(cholesky)/cholesky | solution.py:245
  539.8 10.0 custom-call.67
  553.1 11.7 %cholesky.526 = f32[128,128]{1,0:T(8,128)S(1)} custom-call(f32[128,128]{1,0:T(8,128)S(1)} %cholesky.604), custom_call_target="Cholesky" | custom-call | tf_op jit(solution)/shard_map/jit(cholesky)/cholesky | solution.py:245
  565.5 9.8 custom-call.68
  578.3 11.7 %cholesky.546 = f32[128,128]{1,0:T(8,128)S(1)} custom-call(f32[128,128]{1,0:T(8,128)S(1)} %cholesky.609), custom_call_target="Cholesky" | custom-call | tf_op jit(solution)/shard_map/jit(cholesky)/cholesky | solution.py:245
  591.0 9.8 custom-call.69
  603.5 11.7 %cholesky.564 = f32[128,128]{1,0:T(8,128)S(1)} custom-call(f32[128,128]{1,0:T(8,128)S(1)} %convolution_subtract_fusion.11), custom_call_target="Cholesky" | custom-call | tf_op jit(solution)/shard_map/jit(cholesky)/cholesky | solution.py:245
  624.6 6.8 fusion.5
  631.4 22.4 %while.3 = (s32[]{:T(128)}, f32[1024,1024]{1,0:T(8,128)}, s32[8,2]{0,1:T(2,128)S(1)}, f32[8,128,128]{2,1,0:T(8,128)S(1)}, s32[]{:T(128)}) while((s32[]{:T(128)}, f32[1024,1024]{1,0:T(8,128)}, s32[8,2]{0,1:T(2,128)S(1)}, f32[8,128,128]{2,1,0:T(8,128)S(1)}, s32[]{:T(128)}) %tuple.77), condition=%wide.while_cond.2, body=%wide.while_body.2.sunk | while | flops 2 | bytes 131181 | solution.py:246
  653.8 78.8 %custom-call.70 = f32[8,128,128]{1,2,0:T(8,128)S(1)} custom-call(f32[8,128,128]{2,1,0:T(8,128)S(1)} %get-tuple-element.34), custom_call_target="InvertDiagBlocksLowerTriangular" | custom-call | tf_op jit(solution)/shard_map/jit(_solve_triangular)/triangular_solve | solution.py:246
  751.9 2.8 convolution_subtract_fusion.1
  756.1 3.5 convolution_subtract_fusion.3
  761.1 5.6 reshape.242
  766.7 5.3 copy.66
  772.0 46.2 %convolution_bitcast_fusion = f32[12,2,128,1024]{3,2,0,1:T(8,128)} fusion(f32[2,12,128,4,256]{4,2,1,3,0:T(8,128)} %bitcast.229, f32[4,256,1024,1,1]{2,1,4,0,3:T(8,128)} %bitcast.215), kind=kOutput, calls=%fused_computation.14 | convolution fusion | flops 38654705664 | bytes 29360128 | tf_op jit(solution)/shard_map/fcrw,cwn->frn/dot_general | solution.py:253
  818.1 11.8 %copy.68 = f32[12,2,128,1024]{3,2,1,0:T(8,128)} copy(f32[12,2,128,1024]{3,2,0,1:T(8,128)} %convolution_bitcast_fusion) | data formatting | bytes 25165824 | tf_op jit(solution)/shard_map/transpose | solution.py:263
  831.0 10.7 %fusion = (bf16[3072,1024]{1,0:T(8,128)(2,1)}, bf16[3072,1024]{1,0:T(8,128)(2,1)}) fusion(f32[12,2,128,1024]{3,2,1,0:T(8,128)} %copy.68, pred[3072]{0:T(1024)(128)(4,1)S(1)} %broadcast_bitcast_fusion), kind=kLoop, calls=%fused_computation.7 | loop fusion | flops 15728640 | bytes 25168896 | tf_op jit(solution)/shard_map/convert_element_type | solution.py:16
  841.8 25.2 %bitcast_select_fusion.1 = (f32[12,128,1024]{2,1,0:T(8,128)}, f32[12,128,1024]{2,1,0:T(8,128)S(1)}) fusion(f32[128,1024]{1,0:T(8,128)S(1)} %constant_dynamic-slice_fusion.2, pred[12]{0:T(512)(128)(4,1)S(1)} %add_compare_fusion.1, f32[12,128,4,256]{3,1,0,2:T(8,128)} %bitcast.224, f32[4,256,1024,1]{2,1,3,0:T(8,128)} %bitcast.216), kind=kOutput, calls=%fused_computation.12 | convolution fusion | flops 19330498560 | bytes 23592972 | tf_op jit(solution)/shard_map/crw,cwn->rn/dot_general | solution.py:252
  866.9 4.2 fusion.1
  871.1 81.4 %trailing_base.1.refs_2_ = f32[12,3072,128]{2,1,0:T(8,128)} custom-call(s32[4,12]{1,0:T(4,128)} %select_reduce_fusion.8.refs_0_, s32[4,2]{1,0:T(4,128)} %bitcast.233, s32[1]{0:T(128)} %bitcast.7.refs_2_, f32[12,3072,128]{2,1,0:T(8,128)} %bitcast.227, bf16[1536,1024]{1,0:T(8,128)(2,1)} %get-tuple-element.64.refs_4_, ...), custom_call_target="tpu_custom_call" | custom-call | flops 28991029248 | bytes 60000000 | tf_op jit(solution)/shard_map/trailing_base/pallas_call | solution.py:112
  952.5 17.0 %all-to-all-done.1 = f32[8,4,128,1792]{3,2,1,0:T(8,128)} async-done(((f32[8,4,128,1792]{3,2,1,0:T(8,128)}), f32[8,4,128,1792]{3,2,1,0:T(8,128)}, u32[]{:S(2)}, u32[]{:S(2)}) %all-to-all-start.1) | async-done | bytes 29360160 | tf_op jit(solution)/shard_map/all_to_all | solution.py:201
  969.6 32.7 %extend_add.1 = f32[12,3072,128]{2,1,0:T(8,128)} custom-call(s32[4,12]{1,0:T(4,128)} %select_reduce_fusion.8.refs_0_, s32[4,14]{1,0:T(4,128)} %pad_add_fusion.refs_1_, f32[12,3072,128]{2,1,0:T(8,128)} %trailing_base.1.refs_2_, f32[32,128,1792]{2,1,0:T(8,128)} %bitcast.68.refs_3_.refs_4_.refs_5_.refs_6_, ...), custom_call_target="tpu_custom_call" | custom-call | bytes 70000000 | tf_op jit(solution)/shard_map/extend_add/pallas_call | solution.py:144
  (135 shorter events, 97.9 us)
Async XLA Ops:
  6.5 10.9 %copy-start = (s32[4,64]{1,0:T(4,128)S(1)}, s32[4,64]{1,0:T(4,128)}, u32[]{:S(2)}) copy-start(s32[4,64]{1,0:T(4,128)} %param.6) | copy-start | bytes 3076
  11.7 5.7 copy-start.6
  11.7 95.4 %all-to-all-start = ((f32[8,4,128,256]{3,2,1,0:T(8,128)}), f32[8,4,128,256]{3,2,1,0:T(8,128)}, u32[]{:S(2)}, u32[]{:S(2)}) async-start(f32[8,4,128,256]{3,2,1,0:T(8,128)} %bitcast.217), calls=%async_computation | async-start | bytes 8388608 | tf_op jit(solution)/shard_map/all_to_all | solution.py:201
  17.4 314.5 %all-gather.7.cloned.1.call-start = ((), (), s32[]{:S(2)}) async-start(), calls=%async_computation.2 | async-start | bytes 14155776 | tf_op jit(solution)/shard_map/all_gather | solution.py:228
  114.3 21.6 %copy-start.4 = (f32[12,128,256]{2,1,0:T(8,128)}, f32[12,128,256]{2,1,0:T(8,128)S(1)}, u32[]{:S(2)}) copy-start(f32[12,128,256]{2,1,0:T(8,128)S(1)} %copy_add_fusion) | copy-start | bytes 4718596
  114.3 0.8 collective-permute-start
  115.0 1.2 copy-start.5
  331.9 637.7 %all-to-all-start.1 = ((f32[8,4,128,1792]{3,2,1,0:T(8,128)}), f32[8,4,128,1792]{3,2,1,0:T(8,128)}, u32[]{:S(2)}, u32[]{:S(2)}) async-start(f32[8,4,128,1792]{3,2,1,0:T(8,128)} %bitcast.213), calls=%async_computation.1 | async-start | bytes 58720256 | tf_op jit(solution)/shard_map/all_to_all | solution.py:201
  340.6 38.9 %all-gather.11.cloned.1.call-start = ((), (), s32[]{:S(2)}) async-start(), calls=%async_computation.4 | async-start | bytes 5242880 | tf_op jit(solution)/shard_map/all_gather | solution.py:235
  342.9 498.9 %all-gather.9.cloned.1.call-start = ((), (), s32[]{:S(2)}) async-start(), calls=%async_computation.3 | async-start | bytes 7864320 | tf_op jit(solution)/shard_map/all_gather | solution.py:242
  420.1 2.0 copy-start.3
  732.6 4.7 copy-start.2
  969.6 32.7 %copy-start.1 = (s32[4,64]{1,0:T(4,128)S(1)}, s32[4,64]{1,0:T(4,128)}, u32[]{:S(2)}) copy-start(s32[4,64]{1,0:T(4,128)} %param.6) | copy-start | bytes 3076
Sparse Core Ops, SparseCore 0:
  116.4 215.4 all-gather.6
  343.0 36.4 all-gather.10
  381.1 46.4 all-gather.8

commit v2 on v1

--- a/solution.py
+++ b/solution.py
@@ -135,6 +135,65 @@
     )
 
 
+def across_kernel(in_top_ref, *rest, count, diag_tiles):
+    piece_refs = rest[:count]
+    weight_high, weight_low, high_ref, low_ref = rest[count:]
+    tiles, _, block_size, depth = high_ref.shape
+    rows = tiles * block_size
+    total = jnp.zeros((rows, depth), jnp.float32)
+    for index in range(count):
+        value = piece_refs[index][...].reshape(rows, weight_high.shape[1])
+        high = value.astype(jnp.bfloat16)
+        low = (value - high.astype(jnp.float32)).astype(jnp.bfloat16)
+        for left, right in ((high, weight_high), (high, weight_low), (low, weight_high)):
+            total += jnp.dot(left, right[index], preferred_element_type=jnp.float32)
+    first_tile = pl.program_id(1) * tiles
+    row_ids = lax.broadcasted_iota(jnp.int32, (rows, depth), 0)
+    corner_rows = jnp.where(
+        in_top_ref[pl.program_id(0)] > 0, (diag_tiles - first_tile) * block_size, 0
+    )
+    total = jnp.where(row_ids < corner_rows, 0.0, total)
+    high = total.astype(jnp.bfloat16)
+    high_ref[...] = high.reshape(high_ref.shape)
+    low_ref[...] = (total - high.astype(jnp.float32)).astype(jnp.bfloat16).reshape(low_ref.shape)
+
+
+def make_across(pieces, weights, in_top, tile_rows, diag_tiles):
+    count, fanout, local_rows, width = pieces.shape
+    block_size = local_rows // tile_rows
+    depth = weights[0].shape[2]
+    tiles = next(n for n in (4, 3, 2, 1) if tile_rows % n == 0)
+
+    def piece_spec(index):
+        return pl.BlockSpec(
+            (1, 1, tiles * block_size, width), lambda f, a, *_: (index, f, a, 0)
+        )
+
+    weight_spec = pl.BlockSpec(
+        weights[0].shape, lambda f, a, *_: (0, 0, 0), pipeline_mode=pl.Buffered(1)
+    )
+    out_spec = pl.BlockSpec((tiles, 1, block_size, depth), lambda f, a, *_: (a, f, 0, 0))
+    out_shape = jax.ShapeDtypeStruct((tile_rows, fanout, block_size, depth), jnp.bfloat16)
+    outs = pl.pallas_call(
+        lambda *refs: across_kernel(*refs, count=count, diag_tiles=diag_tiles),
+        grid_spec=pltpu.PrefetchScalarGridSpec(
+            num_scalar_prefetch=1,
+            grid=(fanout, tile_rows // tiles),
+            in_specs=[piece_spec(index) for index in range(count)] + [weight_spec] * 2,
+            out_specs=[out_spec] * 2,
+        ),
+        out_shape=[out_shape] * 2,
+        compiler_params=pltpu.CompilerParams(vmem_limit_bytes=VMEM_LIMIT),
+        cost_estimate=pl.CostEstimate(
+            flops=6 * fanout * local_rows * depth * depth,
+            bytes_accessed=30_000_000,
+            transcendentals=0,
+        ),
+        name="across_rows",
+    )(in_top, *([pieces] * count), *weights)
+    return [out.reshape(tile_rows * fanout * block_size, depth) for out in outs]
+
+
 def make_final(base, slots, row_table, col_table, tile_cols):
     tile_rows = base.shape[0]
     block_size = base.shape[2]
@@ -156,6 +215,34 @@
         cost_estimate=pl.CostEstimate(flops=0, bytes_accessed=70_000_000, transcendentals=0),
         name="extend_add",
     )(row_table, col_table, base, *([slots] * CHILD))
+
+
+def factor_and_inverse(matrix, block_size):
+    size = matrix.shape[0]
+    blocks = size // block_size
+    eye = jnp.eye(block_size, dtype=jnp.float32)
+
+    def multiply(left, right):
+        return jnp.dot(left, right, precision=HIGHEST_PRECISION)
+
+    columns, inverses = [], []
+    trailing = matrix
+    for k in range(blocks):
+        head = lax.linalg.cholesky(trailing[:block_size, :block_size], symmetrize_input=False)
+        inverses.append(lax.linalg.triangular_solve(head, eye, left_side=True, lower=True))
+        below = multiply(trailing[block_size:, :block_size], inverses[k].T)
+        trailing = trailing[block_size:, block_size:] - multiply(below, below.T)
+        above = jnp.zeros((k * block_size, block_size), jnp.float32)
+        columns.append(jnp.concatenate([above, head, below], axis=0))
+    factor = jnp.concatenate(columns, axis=1)
+    inverse = jnp.zeros((0, size), jnp.float32)
+    for k in range(blocks):
+        start, stop = k * block_size, (k + 1) * block_size
+        row = jnp.pad(inverses[k], ((0, 0), (start, size - stop)))
+        if k:
+            row -= multiply(inverses[k], multiply(factor[start:stop, :start], inverse))
+        inverse = jnp.concatenate([inverse, row], axis=0)
+    return factor, inverse
 
 
 def body(front, children, block_map, child_at):
@@ -192,66 +279,93 @@
     )
     place = col_index.astype(jnp.int32).reshape(1)
 
-    def to_rows(parts):
-        packed = jnp.concatenate(parts, axis=1)
+    def to_rows(packed):
         packed = packed.reshape(per_device, grid_rows, block_size, packed.shape[1])
         return packed.transpose(1, 0, 2, 3)
 
     def exchange(packed):
-        got = lax.all_to_all(packed, "row", split_axis=0, concat_axis=0, tiled=True)
-        return got.reshape(slot_rows, block_size, packed.shape[3])
+        return lax.all_to_all(packed, "row", split_axis=0, concat_axis=0, tiled=True)
 
     span = slot_cap * block_size
-    early = exchange(
-        to_rows([children[:, j * span : j * span + block_size] for j in range(panel_tiles)])
-    )
+    early_send = to_rows(
+        jnp.concatenate(
+            [children[:, j * span : j * span + block_size] for j in range(panel_tiles)], axis=1
+        )
+    )
+
     late_send = to_rows(
-        [
-            children[:, j * span + (block_size if j < panel_tiles else 0) : (j + 1) * span]
-            for j in range(fanout)
-        ]
+        jnp.concatenate(
+            [
+                children[:, j * span + (block_size if j < panel_tiles else 0) : (j + 1) * span]
+                for j in range(fanout)
+            ],
+            axis=1,
+        )
     )
     lane_mask = jnp.repeat(in_panel, block_size, axis=1).astype(jnp.float32)
+
+    first = exchange(early_send[:, :1])
+    corner_slots = first[:: slot_cap // per_device, 0]
+    corner_hit = row_hit[:, 0, :diag_tiles].astype(jnp.float32)
+    corner_piece = jnp.sum(
+        corner_hit[:, :, None, None] * (corner_slots * lane_mask[:, None, :])[:, None], axis=0
+    )
+    front_piece = front[:, :, :panel_tiles].reshape(tile_rows, block_size, piece_width)
+    corner_piece = corner_piece + front_piece[:diag_tiles]
+    rest_send = early_send[:, 1:]
+    if per_device > 1:
+        first, rest_send = lax.optimization_barrier((first, rest_send))
+        early = jnp.concatenate([first, exchange(rest_send)], axis=1)
+    else:
+        early = first
+    early = early.reshape(slot_rows, block_size, piece_width)
+
+    corner_pieces = lax.all_gather(corner_piece, ("row", "col"), axis=0, tiled=False)
     masked = early.reshape(CHILD, slot_cap, block_size, piece_width) * lane_mask[:, None, None, :]
     piece = jnp.einsum(
         "cta,ctxw->axw", row_hit.astype(jnp.float32), masked, precision=HIGHEST_PRECISION
     )
-    piece = piece + front[:, :, :panel_tiles].reshape(tile_rows, block_size, piece_width)
-
-    piece = piece.reshape(local_rows, piece_width)
-    turn = [
-        (g * grid_cols + q, ((g // grid_cols) * grid_cols + q) * grid_cols + g % grid_cols)
-        for g in range(grid_rows)
-        for q in range(grid_cols)
-    ]
-    turned = lax.ppermute(piece, ("row", "col"), turn)
-    across_panel = lax.all_gather(turned, "row", axis=0, tiled=False)
-    piece, across_panel, late_send = lax.optimization_barrier((piece, across_panel, late_send))
-    late = exchange(late_send)
-
-    top = across_panel.reshape(fanout, grid_cols, local_rows, piece_width)[
-        :, :, : diag_tiles * block_size
-    ]
-    corner = lax.all_gather(top, "col", axis=0, tiled=False)
-    corner = corner.reshape(
-        grid_cols, fanout, grid_cols, diag_tiles, block_size, panel_tiles, block_size
-    )
-    corner = corner.transpose(3, 1, 0, 4, 5, 2, 6).reshape(
+    piece = (piece + front_piece).reshape(local_rows, piece_width)
+
+    piece, corner_pieces = lax.optimization_barrier((piece, corner_pieces))
+
+    corner = corner_pieces.reshape(grid_rows, grid_cols, diag_tiles, block_size, panel_tiles, block_size)
+    corner = corner.transpose(2, 0, 3, 4, 1, 5).reshape(
         diag_tiles * grid_rows * block_size, panel_width
     )[:panel_width]
+
+    def turned(shift):
+        pairs = []
+        for g in range(grid_rows):
+            part = (g // grid_cols + shift) % fanout
+            for q in range(grid_cols):
+                pairs.append((g * grid_cols + q, (part * grid_cols + q) * grid_cols + g % grid_cols))
+        return lax.ppermute(piece, ("row", "col"), pairs)
+
+    by_shift = [turned(shift) for shift in range(fanout)]
+    part_index = row_index // grid_cols
+    turned_pieces = []
+    for f in range(fanout):
+        chosen = by_shift[0]
+        for shift in range(1, fanout):
+            chosen = jnp.where((part_index - shift) % fanout == f, by_shift[shift], chosen)
+        turned_pieces.append(chosen)
+    turned_pieces = jnp.stack(turned_pieces)
+
+    turned_pieces, piece, late_send = lax.optimization_barrier((turned_pieces, piece, late_send))
+    late = exchange(late_send).reshape(slot_rows, block_size, late_send.shape[3])
     own_panel = lax.all_gather(piece, "col", axis=0, tiled=False)
-    across_panel = across_panel.reshape(fanout, grid_cols, local_rows, piece_width)
-
-    factor = jnp.linalg.cholesky(0.5 * (corner + corner.T))
-    inverse = jax.scipy.linalg.solve_triangular(
-        factor, jnp.eye(panel_width, dtype=jnp.float32), lower=True
-    )
+    turned_pieces, own_panel = lax.optimization_barrier((turned_pieces, own_panel))
+    parts = [[h * grid_cols + q for q in range(grid_cols)] for h in range(fanout)]
+    across_panel = lax.all_gather(
+        turned_pieces, "row", axis=0, tiled=False, axis_index_groups=parts
+    )
+
+    factor, inverse = factor_and_inverse(0.5 * (corner + corner.T), block_size)
     weights = inverse.reshape(panel_width, panel_tiles, grid_cols, block_size)
     weights = weights.transpose(2, 1, 3, 0).reshape(grid_cols, piece_width, panel_width)
 
     own = jnp.einsum("crw,cwn->rn", own_panel, weights, precision=HIGHEST_PRECISION)
-    across = jnp.einsum("fcrw,cwn->frn", across_panel, weights, precision=HIGHEST_PRECISION)
-
     own = own.reshape(tile_rows, block_size, panel_width)
     own_blocks = jnp.arange(tile_rows) * grid_rows + row_index
     own_below = (own_blocks >= PB)[:, None, None]
@@ -260,14 +374,9 @@
     )
     heads = jnp.where(own_below, own, top[None]).reshape(local_rows, panel_width)
     own_halves = split_halves(jnp.where(own_below, own, 0.0).reshape(local_rows, panel_width))
-    across = across.reshape(fanout, tile_rows, block_size, panel_width).transpose(1, 0, 2, 3)
-    across_blocks = jnp.arange(tile_cols) * grid_cols + col_index
-    across = jnp.where(
-        (across_blocks >= PB)[:, None, None],
-        across.reshape(tile_cols, block_size, panel_width),
-        0.0,
-    )
-    across_halves = split_halves(across.reshape(tile_cols * block_size, panel_width))
+    weight_halves = split_halves(weights)
+    in_top = (jnp.arange(fanout) * grid_cols + col_index < PB).astype(jnp.int32)
+    across_halves = make_across(across_panel, weight_halves, in_top, tile_rows, diag_tiles)
 
     flat = front.reshape(tile_rows, block_size * tile_cols, block_size)
     base = make_base(

time: 1020 us -> 992 us (0.973)
  other arithmetic: 301 us -> 229 us
  waiting for transfers between devices: 307 us -> 367 us
  matrix products: 129 us -> 76.2 us
  starting transfers between devices: 15.4 us -> 56.3 us
  local copies, waits for them, and re-layouts: 124 us -> 98.8 us
  Pallas kernels: 114 us -> 139 us
    another operation x33 -> x42, other arithmetic: 257 us -> 198 us  [the longest x24 108 us: factor_and_inverse(): lax.linalg.cholesky(trailing[:block_size, :block_size], symmetrize_input=...]
    all_gather x1, waiting for transfers between devices: 0.01 us -> 52.8 us  [body(): own_panel = lax.all_gather(piece, 'col', axis=0, tiled=False)]
    another operation x29 -> x8, matrix products: 51.4 us -> 2.28 us  [factor_and_inverse(): lax.linalg.triangular_solve(head, eye, left_side=True, lower=True)]
    ppermute x1 -> x2, waiting for transfers between devices: 0.01 us -> 45.7 us  [turned(): return lax.ppermute(piece, ('row', 'col'), pairs)]
    all_to_all x2 -> x3, starting transfers between devices: 14.4 us -> 54.2 us  [exchange(): lax.all_to_all(packed, 'row', split_axis=0, concat_axis=0, tiled=True)]
    all_to_all x2 -> x3, waiting for transfers between devices: 101 us -> 63.2 us  [exchange(): lax.all_to_all(packed, 'row', split_axis=0, concat_axis=0, tiled=True)]
    pallas_call x0 -> x1, Pallas kernels: none -> 26.3 us  [make_across(): pl.pallas_call(lambda *refs: across_kernel(*refs, count=count, diag_tiles...]
    another operation x33 -> x1, local copies, waits for them, and re-layouts: 24.8 us -> 0.01 us  [factor_and_inverse(): lax.linalg.cholesky(trailing[:block_size, :block_size], symmetrize_input=...]
  transfers between devices with their start and end apart: 6 -> 8, of which waited for: 4 -> 6; matrix products, arithmetic and copies ran while one was open for 53% -> 39% of each run, Pallas kernels for 8% -> 11%
where the time goes in v2:
time: 992 us; the launch traced here: 981 us
  waiting for transfers between devices  367 us (37%)
  other arithmetic  229 us (23%)
  Pallas kernels  139 us (14%)
  local copies, waits for them, and re-layouts  98.8 us (10%)
  matrix products  76.2 us (8%)
  starting transfers between devices  56.3 us (6%)
  between operations  14.2 us (1%)
    all_gather x1, waiting for transfers between devices, body(): lax.all_gather(turned_pieces, 'row', axis=0, tiled=False, axis_index_grou...  193 us
    another operation x24, other arithmetic, factor_and_inverse(): lax.linalg.cholesky(trailing[:block_size, :block_size], symmetrize_input=...  108 us
    another operation x16, other arithmetic, factor_and_inverse(): lax.linalg.triangular_solve(head, eye, left_side=True, lower=True)  87.8 us
    pallas_call x1, Pallas kernels, make_base(): pl.pallas_call(lambda *refs: base_kernel(*refs, tile_cols=tile_cols, bloc...  81.3 us
    all_to_all x3, waiting for transfers between devices, exchange(): lax.all_to_all(packed, 'row', split_axis=0, concat_axis=0, tiled=True)  63.2 us
    all_to_all x3, starting transfers between devices, exchange(): lax.all_to_all(packed, 'row', split_axis=0, concat_axis=0, tiled=True)  54.2 us
    all_gather x1, waiting for transfers between devices, body(): own_panel = lax.all_gather(piece, 'col', axis=0, tiled=False)  52.8 us
    ppermute x2, waiting for transfers between devices, turned(): return lax.ppermute(piece, ('row', 'col'), pairs)  45.7 us
  transfers between devices with their start and end apart: 8, of which 6 were waited for; matrix products, arithmetic and copies ran while one was open for 39% of the time, Pallas kernels for 11%

profile of v2, /device:TPU:19, one launch (start us, length us, event | category | flops | bytes accessed | tf_op | source)
XLA Modules:
  0.0 981.1 jit_solution(18119622681583758556)
XLA Ops:
  12.9 5.5 all-to-all-start
  21.6 19.1 %all-to-all-done = f32[8,1,128,256]{3,2,1,0:T(8,128)S(1)} async-done(((f32[8,1,128,256]{3,2,1,0:T(8,128)}), f32[8,1,128,256]{3,2,1,0:T(8,128)S(1)}, u32[]{:S(2)}, u32[]{:S(2)}) %all-to-all-start) | async-done | bytes 1048608 | tf_op jit(solution)/shard_map/all_to_all | solution.py:287
  41.6 3.9 slice.211
  45.5 7.3 all-to-all-start.1
  52.8 4.4 slice.149
  57.2 3.6 copy.84
  60.9 3.0 copy.67
  63.9 19.6 %fusion.136 = (f32[4096,896]{1,0:T(8,128)}, f32[4096,896]{1,0:T(8,128)}) fusion(f32[4096,2048]{1,0:T(8,128)} %param.8), kind=kLoop, calls=%fused_computation.277 | loop fusion | bytes 58720256 | tf_op jit(solution)/shard_map/slice | solution.py:299
  84.5 44.1 %all-to-all-done.1 = f32[8,3,128,256]{3,2,1,0:T(8,128)S(1)} async-done(((f32[8,3,128,256]{3,2,1,0:T(8,128)}), f32[8,3,128,256]{3,2,1,0:T(8,128)S(1)}, u32[]{:S(2)}, u32[]{:S(2)}) %all-to-all-start.1) | async-done | bytes 3145760 | tf_op jit(solution)/shard_map/all_to_all | solution.py:287
  130.6 10.4 %fusion.13 = f32[12,128,256]{2,0,1:T(8,128)S(1)} fusion(f32[4,8,128,256]{3,2,1,0:T(8,128)} %bitcast.200, f32[4,256]{1,0:T(4,128)S(1)} %bitcast.208, s32[4,8]{0,1:T(8,128)S(1)} %copy.59, pred[4,8]{0,1:T(8,128)(4,1)S(1)} %copy.58), kind=kOutput, calls=%fused_computation.31 | convolution fusion | flops 152044288 | bytes 5771424 | tf_op jit(solution)/shard_map/cta,ctxw->axw/dot_general | solution.py:325
  142.0 12.1 %all-gather.6.cloned.1.call-done = f32[32,1,128,256]{3,2,1,0:T(8,128)} async-done(((f32[1,1,128,256]{3,2,1,0:T(8,128)}), f32[32,1,128,256]{3,2,1,0:T(8,128)}) %all-gather.6.cloned.1.call-update) | async-done | bytes 4194320 | tf_op jit(solution)/shard_map/all_gather | solution.py:323
  155.9 10.8 %pad_maximum_fusion = f32[4096,1792]{1,0:T(8,128)S(1)} fusion(f32[4096,896]{1,0:T(8,128)} %get-tuple-element.70, f32[4096,896]{1,0:T(8,128)} %get-tuple-element.69), kind=kLoop, calls=%fused_computation.1 | loop fusion | flops 7340032 | bytes 58720256 | tf_op jit(solution)/shard_map/concatenate | solution.py:297
  166.7 10.0 %copy.100 = f32[4,8,128,1792]{3,2,0,1:T(8,128)} copy(f32[4,8,128,1792]{3,2,1,0:T(8,128)S(1)} %bitcast.183) | data formatting | bytes 58720256 | tf_op jit(solution)/shard_map/reshape | solution.py:283
  176.7 45.6 %collective-permute-done = f32[1536,256]{1,0:T(8,128)S(1)} collective-permute-done((f32[1536,256]{1,0:T(8,128)S(1)}, f32[1536,256]{1,0:T(8,128)S(1)}, u32[]{:S(2)}, u32[]{:S(2)}) %collective-permute-start) | collective-permute-done | bytes 1572896 | tf_op jit(solution)/shard_map/ppermute | solution.py:343
  224.5 41.4 %all-to-all-start.2 = ((f32[8,4,128,1792]{3,2,1,0:T(8,128)}), f32[8,4,128,1792]{3,2,1,0:T(8,128)}, u32[]{:S(2)}, u32[]{:S(2)}) async-start(f32[8,4,128,1792]{3,2,1,0:T(8,128)} %bitcast.182), calls=%async_computation.2 | async-start | bytes 58720256 | tf_op jit(solution)/shard_map/all_to_all | solution.py:287
  266.9 52.8 %all-gather.8.cloned.1.call-done = f32[6144,256]{1,0:T(8,128)} async-done(((f32[1536,256]{1,0:T(8,128)}), f32[6144,256]{1,0:T(8,128)}) %all-gather.8.cloned.1.call-update) | async-done | bytes 6291472 | tf_op jit(solution)/shard_map/all_gather | solution.py:357
  323.1 5.6 copy.71
  328.6 5.2 copy.72
  333.9 3.4 copy.101
  337.4 5.4 copy.73
  342.8 5.0 fusion.2
  349.8 11.7 %custom-call.20 = f32[128,128]{1,0:T(8,128)S(1)} custom-call(f32[128,128]{1,0:T(8,128)S(1)} %slice.213), custom_call_target="Cholesky" | custom-call | tf_op jit(solution)/shard_map/cholesky/custom-call.1 | solution.py:231
  363.5 9.8 custom-call.21
  375.8 4.6 slice_subtract_fusion
  382.0 20.4 %custom-call.22 = f32[128,128]{1,0:T(8,128)S(1)} custom-call(f32[128,128]{1,0:T(8,128)S(1)} %slice.216), custom_call_target="Cholesky" | custom-call | tf_op jit(solution)/shard_map/cholesky/custom-call.1 | solution.py:231
  404.5 9.8 custom-call.23
  416.7 3.8 slice_subtract_fusion.1
  420.5 11.7 %custom-call.24 = f32[128,128]{1,0:T(8,128)S(1)} custom-call(f32[128,128]{1,0:T(8,128)S(1)} %slice.220), custom_call_target="Cholesky" | custom-call | tf_op jit(solution)/shard_map/cholesky/custom-call.1 | solution.py:231
  434.1 10.0 %custom-call.25 = f32[1,128,128]{1,2,0:T(8,128)S(1)} custom-call(f32[1,128,128]{2,1,0:T(8,128)S(1)} %get-tuple-element.61), custom_call_target="InvertDiagBlocksLowerTriangular" | custom-call | tf_op jit(solution)/shard_map/triangular_solve/custom-call.0 | solution.py:232
  448.1 11.7 %custom-call.26 = f32[128,128]{1,0:T(8,128)S(1)} custom-call(f32[128,128]{1,0:T(8,128)S(1)} %slice.223), custom_call_target="Cholesky" | custom-call | tf_op jit(solution)/shard_map/cholesky/custom-call.1 | solution.py:231
  461.8 9.8 custom-call.27
  476.1 12.1 %custom-call.28 = f32[128,128]{1,0:T(8,128)S(1)} custom-call(f32[128,128]{1,0:T(8,128)S(1)} %slice.226), custom_call_target="Cholesky" | custom-call | tf_op jit(solution)/shard_map/cholesky/custom-call.1 | solution.py:231
  490.2 9.8 custom-call.29
  501.3 11.7 %custom-call.30 = f32[128,128]{1,0:T(8,128)S(1)} custom-call(f32[128,128]{1,0:T(8,128)S(1)} %slice.229), custom_call_target="Cholesky" | custom-call | tf_op jit(solution)/shard_map/cholesky/custom-call.1 | solution.py:231
  515.0 9.9 %custom-call.31 = f32[1,128,128]{1,2,0:T(8,128)S(1)} custom-call(f32[1,128,128]{2,1,0:T(8,128)S(1)} %get-tuple-element.55), custom_call_target="InvertDiagBlocksLowerTriangular" | custom-call | tf_op jit(solution)/shard_map/triangular_solve/custom-call.0 | solution.py:232
  525.9 11.7 %custom-call.32 = f32[128,128]{1,0:T(8,128)S(1)} custom-call(f32[128,128]{1,0:T(8,128)S(1)} %slice.233), custom_call_target="Cholesky" | custom-call | tf_op jit(solution)/shard_map/cholesky/custom-call.1 | solution.py:231
  539.0 9.8 custom-call.33
  549.7 11.7 %custom-call.34 = f32[128,128]{1,0:T(8,128)S(1)} custom-call(f32[128,128]{1,0:T(8,128)S(1)} %convolution_subtract_fusion.10), custom_call_target="Cholesky" | custom-call | tf_op jit(solution)/shard_map/cholesky/custom-call.1 | solution.py:231
  562.7 10.0 %custom-call.35 = f32[1,128,128]{1,2,0:T(8,128)S(1)} custom-call(f32[1,128,128]{2,1,0:T(8,128)S(1)} %get-tuple-element.51), custom_call_target="InvertDiagBlocksLowerTriangular" | custom-call | tf_op jit(solution)/shard_map/triangular_solve/custom-call.0 | solution.py:232
  596.0 5.6 reshape.203
  601.6 5.3 copy.74
  608.8 5.2 fusion.1
  614.1 24.2 %bitcast_select_fusion = (f32[12,128,1024]{2,1,0:T(8,128)}, f32[12,128,1024]{2,1,0:T(8,128)S(1)}) fusion(f32[128,1024]{1,0:T(8,128)S(1)} %constant_dynamic-slice_fusion.1, pred[12]{0:T(512)(128)(4,1)S(1)} %copy-done.29, f32[12,128,4,256]{3,1,0,2:T(8,128)} %bitcast.196, f32[4,256,1024,1]{2,1,3,0:T(8,128)S(1)} %bitcast.184), kind=kOutput, calls=%fused_computation.6 | convolution fusion | flops 19330498560 | bytes 23592972 | tf_op jit(solution)/shard_map/crw,cwn->rn/dot_general | solution.py:368
  638.3 4.3 fusion
  642.5 192.7 %all-gather.10.cloned.1.call-done = f32[8,1536,256]{2,1,0:T(8,128)} async-done(((f32[2,1536,256]{2,1,0:T(8,128)}), f32[8,1536,256]{2,1,0:T(8,128)}) %all-gather.10.cloned.1.call-update) | async-done | bytes 12582928 | tf_op jit(solution)/shard_map/all_gather | solution.py:360
  835.3 26.3 %across_rows.1 = (bf16[12,2,128,1024]{3,2,1,0:T(8,128)(2,1)}, bf16[12,2,128,1024]{3,2,1,0:T(8,128)(2,1)}) custom-call(s32[2]{0:T(128)} %compare_convert_fusion.refs_0_, f32[4,2,1536,256]{3,2,1,0:T(8,128)} %bitcast.211, f32[4,2,1536,256]{3,2,1,0:T(8,128)} %bitcast.212, f32[4,2,1536,256]{3,2,1,0:T(8,128)} %bitcast.213, f32[4,2,1536,256]{3,2,1,0:T(8,128)} %bitcast.214, ...), custom_call_target="tpu_custom_call" | custom-call | flops 19327352832 | bytes 30000000 | tf_op jit(solution)/shard_map/across_rows/pallas_call | solution.py:177
  861.6 81.3 %trailing_base.1.refs_2_ = f32[12,3072,128]{2,1,0:T(8,128)} custom-call(s32[4,12]{1,0:T(4,128)} %copy.77.refs_0_, s32[4,2]{1,0:T(4,128)} %bitcast.210, s32[1]{0:T(128)} %bitcast.7.refs_2_, f32[12,3072,128]{2,1,0:T(8,128)} %bitcast.205, bf16[1536,1024]{1,0:T(8,128)(2,1)} %get-tuple-element.76.refs_4_, bf16[1536,1024]{1,0:T(8,128)(2,1)} %get-tuple-element.75.refs_5_, ...), custom_call_target="tpu_custom_call" | custom-call | flops 28991029248 | bytes 60000000 | tf_op jit(solution)/shard_map/trailing_base/pallas_call | solution.py:112
  942.9 31.5 %extend_add.1 = f32[12,3072,128]{2,1,0:T(8,128)} custom-call(s32[4,12]{1,0:T(4,128)} %copy.77.refs_0_, s32[4,14]{1,0:T(4,128)} %pad_add_fusion.refs_1_, f32[12,3072,128]{2,1,0:T(8,128)} %trailing_base.1.refs_2_, f32[32,128,1792]{2,1,0:T(8,128)} %bitcast.59.refs_3_.refs_4_.refs_5_.refs_6_, f32[32,128,1792]{2,1,0:T(8,128)} %bitcast.59.refs_3_.refs_4_.refs_5_.refs_6_, ...), custom_call_target="tpu_custom_call" | custom-call | bytes 70000000 | tf_op jit(solution)/shard_map/extend_add/pallas_call | solution.py:203
  (200 shorter events, 82.0 us)
Async XLA Ops:
  6.5 12.0 %copy-start = (s32[4,64]{1,0:T(4,128)S(1)}, s32[4,64]{1,0:T(4,128)}, u32[]{:S(2)}) copy-start(s32[4,64]{1,0:T(4,128)} %param.9) | copy-start | bytes 3076
  9.8 2.0 copy-start.4
  9.8 8.7 copy-start.30
  12.9 27.8 %all-to-all-start = ((f32[8,1,128,256]{3,2,1,0:T(8,128)}), f32[8,1,128,256]{3,2,1,0:T(8,128)S(1)}, u32[]{:S(2)}, u32[]{:S(2)}) async-start(f32[8,1,128,256]{3,2,1,0:T(8,128)} %slice.210), calls=%async_computation | async-start | bytes 2097152 | tf_op jit(solution)/shard_map/all_to_all | solution.py:287
  18.5 135.6 %all-gather.6.cloned.1.call-start = ((), (), s32[]{:S(2)}) async-start(), calls=%async_computation.3 | async-start | bytes 4325376 | tf_op jit(solution)/shard_map/all_gather | solution.py:323
  40.7 4.8 copy-start.7
  45.5 83.1 %all-to-all-start.1 = ((f32[8,3,128,256]{3,2,1,0:T(8,128)}), f32[8,3,128,256]{3,2,1,0:T(8,128)S(1)}, u32[]{:S(2)}, u32[]{:S(2)}) async-start(f32[8,3,128,256]{3,2,1,0:T(8,128)} %slice.211), calls=%async_computation.1 | async-start | bytes 6291456 | tf_op jit(solution)/shard_map/all_to_all | solution.py:287
  63.9 19.6 %copy-start.8 = (f32[8,1,128,256]{3,2,1,0:T(8,128)S(1)}, f32[8,1,128,256]{3,2,1,0:T(8,128)}, u32[]{:S(2)}) copy-start(f32[8,1,128,256]{3,2,1,0:T(8,128)} %copy-done.7) | copy-start | bytes 3145732
  130.6 10.5 %copy-start.10 = (f32[12,128,256]{2,1,0:T(8,128)S(1)}, f32[12,128,256]{2,1,0:T(8,128)}, u32[]{:S(2)}) copy-start(f32[12,128,256]{2,1,0:T(8,128)} %copy.67) | copy-start | bytes 4718596
  142.0 24.7 %copy-start.9 = (f32[12,128,256]{2,1,0:T(8,128)}, f32[12,128,256]{2,1,0:T(8,128)S(1)}, u32[]{:S(2)}) copy-start(f32[12,128,256]{2,1,0:T(8,128)S(1)} %copy_add_fusion) | copy-start | bytes 4718596
  154.1 68.3 %collective-permute-start = (f32[1536,256]{1,0:T(8,128)S(1)}, f32[1536,256]{1,0:T(8,128)S(1)}, u32[]{:S(2)}, u32[]{:S(2)}) collective-permute-start(f32[1536,256]{1,0:T(8,128)S(1)} %bitcast.193), channel_id=1, source_target_pairs={{0,16},{1,20},{2,24},{3,28},{4,17},{5,21},{6,25},{7,29},{8,18},{9,... | collective-permute-start | bytes 4718600 | tf_op jit(solution)/shard_map/ppermute | solution.py:343
  155.1 67.2 %collective-permute-start.1 = (f32[1536,256]{1,0:T(8,128)S(1)}, f32[1536,256]{1,0:T(8,128)S(1)}, u32[]{:S(2)}, u32[]{:S(2)}) collective-permute-start(f32[1536,256]{1,0:T(8,128)S(1)} %bitcast.194), channel_id=1, source_target_pairs={{0,0},{1,4},{2,8},{3,12},{4,1},{5,5},{6,9},{7,13},{8,2},{9,6},{10,... | collective-permute-start | bytes 4718600 | tf_op jit(solution)/shard_map/ppermute | solution.py:343
  224.5 718.3 %all-to-all-start.2 = ((f32[8,4,128,1792]{3,2,1,0:T(8,128)}), f32[8,4,128,1792]{3,2,1,0:T(8,128)}, u32[]{:S(2)}, u32[]{:S(2)}) async-start(f32[8,4,128,1792]{3,2,1,0:T(8,128)} %bitcast.182), calls=%async_computation.2 | async-start | bytes 58720256 | tf_op jit(solution)/shard_map/all_to_all | solution.py:287
  265.9 53.8 %all-gather.8.cloned.1.call-start = ((), (), s32[]{:S(2)}) async-start(), calls=%async_computation.4 | async-start | bytes 7864320 | tf_op jit(solution)/shard_map/all_gather | solution.py:357
  266.6 568.6 %all-gather.10.cloned.1.call-start = ((), (), s32[]{:S(2)}) async-start(), calls=%async_computation.5 | async-start | bytes 15728640 | tf_op jit(solution)/shard_map/all_gather | solution.py:360
  333.9 3.5 copy-start.3
  347.8 2.0 copy-start.5
  373.6 0.6 copy-start.14
  380.4 1.7 copy-start.6
  414.6 0.6 copy-start.19
  444.4 0.6 copy-start.21
  447.0 1.2 copy-start.11
  471.9 0.6 copy-start.17
  473.8 98.9 %copy-start.15 = (f32[128,128]{1,0:T(8,128)S(1)}, f32[128,128]{1,0:T(8,128)}, u32[]{:S(2)}) copy-start(f32[128,128]{1,0:T(8,128)} %copy-done.14) | copy-start | bytes 196612
  500.3 24.6 %copy-start.23 = (f32[128,128]{1,0:T(8,128)}, f32[128,128]{1,0:T(8,128)S(1)}, u32[]{:S(2)}) copy-start(f32[128,128]{1,0:T(8,128)S(1)} %fusion.78) | copy-start | bytes 196612
  501.3 72.9 %copy-start.20 = (f32[128,128]{1,0:T(8,128)S(1)}, f32[128,128]{1,0:T(8,128)}, u32[]{:S(2)}) copy-start(f32[128,128]{1,0:T(8,128)} %copy-done.19) | copy-start | bytes 196612
  549.1 26.6 %copy-start.12 = (f32[128,128]{1,0:T(8,128)S(1)}, f32[128,128]{1,0:T(8,128)}, u32[]{:S(2)}) copy-start(f32[128,128]{1,0:T(8,128)} %get-tuple-element.66) | copy-start | bytes 196612
  549.1 26.6 %copy-start.13 = (f32[128,128]{1,0:T(8,128)S(1)}, f32[128,128]{1,0:T(8,128)}, u32[]{:S(2)}) copy-start(f32[128,128]{1,0:T(8,128)} %get-tuple-element.64) | copy-start | bytes 196612
  573.8 2.6 copy-start.22
  575.7 2.3 copy-start.16
  576.4 2.7 copy-start.18
  577.9 2.7 copy-start.26
  582.1 0.8 copy-start.27
  582.3 0.9 copy-start.25
  582.5 1.2 copy-start.24
  583.6 5.1 copy-start.28
  608.8 5.3 copy-start.2
  608.8 5.3 copy-start.29
  942.9 31.5 %copy-start.1 = (s32[4,64]{1,0:T(4,128)S(1)}, s32[4,64]{1,0:T(4,128)}, u32[]{:S(2)}) copy-start(s32[4,64]{1,0:T(4,128)} %param.9) | copy-start | bytes 3076
Sparse Core Ops, SparseCore 0:
  41.8 112.2 all-gather.5
  268.3 51.3 all-gather.7
  321.3 513.9 all-gather.9
